TPU v7x, 512 devices: a whole 4x8x8 slice. The times are simulated.
512 devices in a mesh: leaf: 64 (over z, y), grp: 8 (over x, core).
Axes of the slice: x: 4, y: 8, z: 8, core: 2. Of those that a mesh axis runs over, the one named last changes fastest.
Arguments:
- vectors: bfloat16 [4096, 256, 16], P(('leaf', 'grp')), may hold values from -6 to 6
- leaf_basis: bfloat16 [4096, 256, 64], P(('leaf', 'grp')), may hold values from -0.375 to 0.375
- transfer: float32 [512, 15, 64, 64], P(('leaf', 'grp')), may hold values from -0.5 to 0.5
- couple_src: int32 [512, 12, 3], P(('leaf', 'grp')), may hold values from 0 to 4095, as said below
- couple_mat: float32 [512, 12, 3, 64, 64], P(('leaf', 'grp')), may hold values from -0.4375 to 0.4375
- root_src: int32 [64, 4], P('leaf'), may hold values from 0 to 63, as said below
- root_mat: float32 [64, 4, 64, 64], P('leaf'), may hold values from -0.375 to 0.375
- near_src: int32 [4096, 3], P(('leaf', 'grp')), may hold values from 0 to 4095, as said below
- near_blocks: bfloat16 [4096, 256, 3, 256], P(('leaf', 'grp')), may hold values from -0.21875 to 0.21875
Outputs:
- product: float32 [4096, 256, 16], P(('leaf', 'grp'))
Inputs may be any that keep to these rules, and one draw needn't show every extreme that they name: `couple_src`: rows of each block d hold the levels 0, 1, ... in order, 8, 4, ... rows down to 4; entry [d, r, j] names a cluster of row r's level 2 or 3 places from row r's cluster on the cycle of that level's clusters (the last followed by the first); a row's three entries are distinct. `root_src`: each entry names another top cluster neither equal nor next to the row's own on the cycle of 64 top clusters; a row's entries are distinct. `near_src`: entry [t, 0] is t itself; the other two are distinct leaves 1 or 2 places from t on the cycle of 4096 leaves.
All inputs are finite; a program needn't handle non-finite values.
Results may differ from a plain program's by a relative error of at most 0.0019.
Values may be sent and summed in bfloat16 or wider, within the bound.
A program may use at most 64 MiB of HBM per device.

v0:
```python
import jax
import jax.numpy as jnp
from jax import lax
from jax.sharding import PartitionSpec as P

highest = lax.Precision.HIGHEST


def extended_2(array, sides, width):
    for axis, dim in sides:
        count, length = (lax.axis_size(axis), array.shape[dim])
        up = [(i, (i + 1) % count) for i in range(count)]
        down = [(j, i) for i, j in up]
        last = lax.slice_in_dim(array, length - width, length, axis=dim)
        initial = lax.slice_in_dim(array, 0, width, axis=dim)
        before = lax.ppermute(last, axis, up)
        after = lax.ppermute(initial, axis, down)
        array = jnp.concatenate([before, array, after], axis=dim)
    return array


def level_halo(coeff_level):
    return extended_2(coeff_level, ((("leaf", "grp"), 0),), 3)


def body(
    vectors, leaf_basis, transfer, couple_src, couple_mat, root_src, root_mat, near_src, near_blocks
):
    per_device = vectors.shape[0]
    levels = per_device.bit_length() - 1
    cycle_size = lax.axis_size(("leaf", "grp"))
    device = lax.axis_index(("leaf", "grp"))
    extended = extended_2(vectors, ((("leaf", "grp"), 0),), 2)
    places = jnp.mod(near_src - device * per_device + 2, per_device * cycle_size)
    picked = extended[places]
    nearby = jnp.einsum("tmen,tenv->tmv", near_blocks, picked, preferred_element_type=jnp.float32)
    coeffs = [jnp.einsum("tmv,tmk->tvk", vectors, leaf_basis, preferred_element_type=jnp.float32)]
    for height in range(1, levels + 1):
        clusters = per_device >> height - 1
        offset = 2 * per_device - 2 * clusters
        children = jnp.einsum(
            "cvk,ckl->cvl", coeffs[-1], transfer[0, offset : offset + clusters], precision=highest
        )
        coeffs.append(
            children.reshape(clusters // 2, 2, children.shape[1], children.shape[2]).sum(axis=1)
        )
    extended_levels = [level_halo(coeffs[height]) for height in range(levels - 1)]
    couplings = []
    for height in range(levels - 1):
        clusters = per_device >> height
        offset = 2 * per_device - 2 * clusters
        sources = couple_src[0, offset : offset + clusters]
        positions = jnp.mod(sources - device * clusters + 3, clusters * cycle_size)
        gathered = extended_levels[height][positions]
        couplings.append(
            jnp.einsum(
                "tcvk,tckl->tvl",
                gathered,
                couple_mat[0, offset : offset + clusters],
                precision=highest,
            )
        )
    device_up = transfer[0, 2 * per_device - 2]
    lifted = jnp.dot(
        coeffs[levels][0], device_up, precision=highest, preferred_element_type=jnp.float32
    )
    group_total = lax.psum(lifted, "grp")
    tops = lax.all_gather(group_total[None], "leaf", axis=0, tiled=True)
    top_down = jnp.einsum("cvk,ckl->vl", tops[root_src[0]], root_mat[0], precision=highest)
    downward = jnp.einsum("vl,kl->vk", top_down, device_up, precision=highest)[None]
    for height in range(levels, 0, -1):
        clusters = per_device >> height - 1
        offset = 2 * per_device - 2 * clusters
        spread = jnp.repeat(downward, 2, axis=0)
        downward = jnp.einsum(
            "cvl,ckl->cvk", spread, transfer[0, offset : offset + clusters], precision=highest
        )
        if height - 1 <= levels - 2:
            downward = downward + couplings[height - 1]
    rounded = downward.astype(jnp.bfloat16)
    distant = jnp.einsum("tmk,tvk->tmv", leaf_basis, rounded, preferred_element_type=jnp.float32)
    return distant + nearby


def solution(mesh):
    in_specs = (
        P(("leaf", "grp"), None, None),
        P(("leaf", "grp"), None, None),
        P(("leaf", "grp"), None, None, None),
        P(("leaf", "grp"), None, None),
        P(("leaf", "grp"), None, None, None, None),
        P("leaf", None),
        P("leaf", None, None, None),
        P(("leaf", "grp"), None),
        P(("leaf", "grp"), None, None, None),
    )
    out_specs = P(("leaf", "grp"), None, None)
    return jax.shard_map(body, mesh=mesh, in_specs=in_specs, out_specs=out_specs, check_vma=False)
```

profile of v0, /device:TPU:1, one launch (start us, length us, event | category | flops | bytes accessed | tf_op | source)
XLA Modules:
  0.0 134.8 jit_solution(14163096036735941828)
XLA Ops:
  0.0 1.3 fusion.38
  1.3 1.3 bitcast_reduce_fusion
  2.7 4.5 %collective-permute-start = (f32[3,16,64]{2,1,0:T(8,128)S(1)}, f32[3,16,64]{2,1,0:T(8,128)S(1)}, u32[]{:S(2)}, u32[]{:S(2)}) collective-permute-start(f32[3,16,64]{2,1,0:T(8,128)S(1)} %get-tuple-element.9), channel_id=1, source_target_pairs={{0,1},{1,2},{2,3},{3,4},{4,5},{5,6},{6,7},{7,8},{8,9},{9,10},{10,1... | collective-permute-start | bytes 36872 | tf_op jit(solution)/shard_map/ppermute | solution.py:16
  7.2 6.2 %collective-permute-start.1 = (f32[3,16,64]{2,1,0:T(8,128)S(1)}, f32[3,16,64]{2,1,0:T(8,128)S(1)}, u32[]{:S(2)}, u32[]{:S(2)}) collective-permute-start(f32[3,16,64]{2,1,0:T(8,128)S(1)} %get-tuple-element.10), channel_id=1, source_target_pairs={{1,0},{2,1},{3,2},{4,3},{5,4},{6,5},{7,6},{8,7},{9,8},{10,9},{11,1... | collective-permute-start | bytes 36872 | tf_op jit(solution)/shard_map/ppermute | solution.py:17
  13.4 0.6 fusion.36
  14.0 1.9 %collective-permute-start.2 = (f32[3,16,64]{2,1,0:T(8,128)}, f32[3,16,64]{2,1,0:T(8,128)}, u32[]{:S(2)}, u32[]{:S(2)}) collective-permute-start(f32[3,16,64]{2,1,0:T(8,128)} %get-tuple-element.7), channel_id=1, source_target_pairs={{0,1},{1,2},{2,3},{3,4},{4,5},{5,6},{6,7},{7,8},{8,9},{9,10},{10,1... | collective-permute-start | bytes 36872 | tf_op jit(solution)/shard_map/ppermute | solution.py:16
  15.9 10.1 %collective-permute-start.3 = (f32[3,16,64]{2,1,0:T(8,128)}, f32[3,16,64]{2,1,0:T(8,128)}, u32[]{:S(2)}, u32[]{:S(2)}) collective-permute-start(f32[3,16,64]{2,1,0:T(8,128)} %get-tuple-element.8), channel_id=1, source_target_pairs={{1,0},{2,1},{3,2},{4,3},{5,4},{6,5},{7,6},{8,7},{9,8},{10,9},{11,1... | collective-permute-start | bytes 36872 | tf_op jit(solution)/shard_map/ppermute | solution.py:17
  26.0 1.3 fusion.35
  27.4 1.9 %collective-permute-start.4 = (bf16[2,256,16]{1,2,0:T(8,128)(2,1)}, bf16[2,256,16]{1,2,0:T(8,128)(2,1)}, u32[]{:S(2)}, u32[]{:S(2)}) collective-permute-start(bf16[2,256,16]{1,2,0:T(8,128)(2,1)} %get-tuple-element.5), channel_id=1, source_target_pairs={{0,1},{1,2},{2,3},{3,4},{4,5},{5,6},{6,7},{7,8},{8,9},{9,10},{10,1... | collective-permute-start | bytes 49160 | tf_op jit(solution)/shard_map/ppermute | solution.py:16
  29.3 1.1 bitcast_reduce_fusion.1
  30.4 0.8 compare_select_fusion.1
  31.2 0.1 copy.16
  31.3 0.1 reshape.179
  31.4 0.6 pad_clamp_fusion.2
  32.0 1.0 convolution_bitcast_fusion.5
  33.0 0.9 convolution_bitcast_fusion.4
  33.9 19.1 %psum.7 = f32[1,16,64]{2,1,0:T(8,128)S(1)} all-reduce(f32[1,16,64]{2,1,0:T(8,128)S(1)} %convolution_bitcast_fusion.4), channel_id=1, replica_groups=mesh['leaf'=64,'grp'=8] {'grp'}, use_global_device_ids=true, to_apply=%region_2.3 | all-reduce | flops 1024 | bytes 8192 | tf_op jit(solution)/shard_map/psum | solution.py:67
  53.1 41.4 %all_gather.3 = f32[64,16,64]{2,1,0:T(8,128)} all-gather(f32[1,16,64]{2,1,0:T(8,128)S(1)} %psum.7), channel_id=1, replica_groups=mesh['leaf'=64,'grp'=8] {'leaf'}, dimensions={0}, use_global_device_ids=true | all-gather | bytes 266240 | tf_op jit(solution)/shard_map/all_gather | solution.py:68
  94.6 1.6 %gather_fusion = f32[4,16,64]{2,1,0:T(8,128)S(1)} fusion(f32[64,16,64]{2,1,0:T(8,128)} %all_gather.3, s32[1024]{0:T(1024)S(1)} %pad_clamp_fusion.3), kind=kCustom, calls=%fused_computation | custom fusion | bytes 32784 | tf_op jit(solution)/shard_map/gather | solution.py:69
  96.2 0.2 convolution_bitcast_fusion.3
  96.4 0.9 fusion.25
  97.3 1.7 %fusion.20 = f32[2,16,64]{2,1,0:T(8,128)} fusion(f32[1,15,64,64]{3,2,1,0:T(8,128)} %param.11, f32[16,64]{1,0:T(8,128)S(1)} %fusion.25), kind=kOutput, calls=%fused_computation.34 | convolution fusion | flops 1572864 | bytes 77824 | tf_op jit(solution)/shard_map/cvl,ckl->cvk/dot_general | solution.py:75
  99.0 0.1 copy.17
  99.1 0.1 reshape.187
  99.2 0.6 pad_clamp_fusion.1
  99.8 0.1 copy.18
  99.9 0.1 reshape.195
  99.9 0.6 pad_clamp_fusion
  100.5 0.0 collective-permute-done
  100.6 17.2 %collective-permute-start.5 = (bf16[2,256,16]{1,2,0:T(8,128)(2,1)}, bf16[2,256,16]{1,2,0:T(8,128)(2,1)}, u32[]{:S(2)}, u32[]{:S(2)}) collective-permute-start(bf16[2,256,16]{1,2,0:T(8,128)(2,1)} %get-tuple-element.6), channel_id=1, source_target_pairs={{1,0},{2,1},{3,2},{4,3},{5,4},{6,5},{7,6},{8,7},{9,8},{10,9},{11,1... | collective-permute-start | bytes 49160 | tf_op jit(solution)/shard_map/ppermute | solution.py:17
  117.8 0.0 collective-permute-done.1
  117.8 0.0 copy-start.1
  117.8 1.5 %gather_fusion.1 = f32[12,16,64]{2,1,0:T(8,128)} fusion(f32[10,16,64]{2,1,0:T(8,128)S(1)} %pad_maximum_fusion.2, s32[1024]{0:T(1024)} %pad_clamp_fusion.2), kind=kCustom, calls=%fused_computation.1 | custom fusion | bytes 98352 | tf_op jit(solution)/shard_map/gather | solution.py:54
  119.3 1.5 %convolution_bitcast_fusion.2 = f32[4,16,64]{2,1,0:T(8,128)S(1)} fusion(f32[4,3,16,64]{3,2,1,0:T(8,128)} %bitcast.97, f32[1,12,3,64,64]{4,3,2,1,0:T(8,128)} %param.13), kind=kOutput, calls=%fused_computation.11 | convolution fusion | flops 9437184 | bytes 507904 | tf_op jit(solution)/shard_map/tcvk,tckl->tvl/dot_general | solution.py:56
  120.8 0.7 broadcast_in_dim.18
  121.6 1.2 convolution_add_fusion
  122.8 1.5 %fusion.8 = f32[8,16,64]{2,1,0:T(8,128)S(1)} fusion(f32[8,16,64]{2,1,0:T(8,128)S(1)} %bitcast.98, f32[1,15,64,64]{3,2,1,0:T(8,128)} %param.11), kind=kOutput, calls=%fused_computation.19 | convolution fusion | flops 6291456 | bytes 327680 | tf_op jit(solution)/shard_map/cvl,ckl->cvk/dot_general | solution.py:75
  124.3 0.0 collective-permute-done.2
  124.3 0.0 collective-permute-done.3
  124.3 1.4 %pad_maximum_fusion = f32[14,16,64]{2,1,0:T(8,128)} fusion(f32[3,16,64]{2,1,0:T(8,128)} %collective-permute-done.3, f32[8,16,64]{2,1,0:T(8,128)S(1)} %fusion.38, f32[3,16,64]{2,1,0:T(8,128)} %collective-permute-done.2), kind=kLoop, calls=%fused_computation.31 | loop fusion | flops 28672 | bytes 114688 | tf_op jit(solution)/shard_map/concatenate | solution.py:18
  125.7 2.3 %gather_fusion.2 = f32[24,16,64]{2,1,0:T(8,128)} fusion(f32[14,16,64]{2,1,0:T(8,128)} %pad_maximum_fusion, s32[1024]{0:T(1024)} %pad_clamp_fusion.1), kind=kCustom, calls=%fused_computation.2 | custom fusion | bytes 196704 | tf_op jit(solution)/shard_map/gather | solution.py:54
  127.9 2.0 %fusion.3 = bf16[8,16,64]{2,1,0:T(8,128)(2,1)S(1)} fusion(f32[8,16,64]{2,1,0:T(8,128)S(1)} %fusion.8, f32[8,3,16,64]{3,2,1,0:T(8,128)} %bitcast.96, f32[1,12,3,64,64]{4,3,2,1,0:T(8,128)} %param.13), kind=kOutput, calls=%fused_computation.9 | convolution fusion | flops 18890752 | bytes 1032192 | tf_op jit(solution)/shard_map/tcvk,tckl->tvl/dot_general | solution.py:56
  130.0 0.0 copy-done.1
  130.0 0.8 fusion.39
  130.8 0.0 collective-permute-done.4
  130.8 0.9 pad_maximum_fusion.1
  131.7 0.6 gather_fusion.3
  132.3 2.5 %fusion.1 = f32[8,256,16]{1,2,0:T(8,128)} fusion(f32[8,16,256]{2,1,0:T(8,128)} %fusion.39, bf16[8,3,256,16]{2,3,1,0:T(8,128)(2,1)S(1)} %bitcast.95, bf16[8,256,3,256]{3,1,2,0:T(8,128)(2,1)S(1)} %copy-done), kind=kOutput, calls=%fused_computation.6 | convolution fusion | flops 50364416 | bytes 3604480 | tf_op jit(solution)/shard_map/tmen,tenv->tmv/dot_general | solution.py:36
  (20 shorter events, 0.1 us)
Async XLA Ops:
  0.0 132.3 %copy-start = (bf16[8,256,3,256]{3,1,2,0:T(8,128)(2,1)S(1)}, bf16[8,256,3,256]{3,1,2,0:T(8,128)(2,1)}, u32[]{:S(2)}) copy-start(bf16[8,256,3,256]{3,1,2,0:T(8,128)(2,1)} %param.17) | copy-start | bytes 9437188
  0.0 99.0 %copy-start.4 = (s32[1,12,3]{1,0,2:T(1,128)S(1)}, s32[1,12,3]{1,0,2:T(1,128)}, u32[]{:S(2)}) copy-start(s32[1,12,3]{1,0,2:T(1,128)} %param.12) | copy-start | bytes 436
  0.0 94.5 %copy-start.6 = (s32[1,4]{1,0:T(1,128)S(1)}, s32[1,4]{1,0:T(1,128)}, u32[]{:S(2)}) copy-start(s32[1,4]{1,0:T(1,128)} %param.14) | copy-start | bytes 52
  0.0 96.1 %copy-start.2 = (f32[1,4,64,64]{3,2,1,0:T(8,128)S(1)}, f32[1,4,64,64]{3,2,1,0:T(8,128)}, u32[]{:S(2)}) copy-start(f32[1,4,64,64]{3,2,1,0:T(8,128)} %param.15) | copy-start | bytes 196612
  0.0 99.7 %copy-start.5 = (s32[8,3]{0,1:T(4,128)S(1)}, s32[8,3]{0,1:T(4,128)}, u32[]{:S(2)}) copy-start(s32[8,3]{0,1:T(4,128)} %param.16) | copy-start | bytes 292
  2.7 97.9 %collective-permute-start = (f32[3,16,64]{2,1,0:T(8,128)S(1)}, f32[3,16,64]{2,1,0:T(8,128)S(1)}, u32[]{:S(2)}, u32[]{:S(2)}) collective-permute-start(f32[3,16,64]{2,1,0:T(8,128)S(1)} %get-tuple-element.9), channel_id=1, source_target_pairs={{0,1},{1,2},{2,3},{3,4},{4,5},{5,6},{6,7},{7,8},{8,9},{9,10},{10,1... | collective-permute-start | bytes 36872 | tf_op jit(solution)/shard_map/ppermute | solution.py:16
  7.2 110.6 %collective-permute-start.1 = (f32[3,16,64]{2,1,0:T(8,128)S(1)}, f32[3,16,64]{2,1,0:T(8,128)S(1)}, u32[]{:S(2)}, u32[]{:S(2)}) collective-permute-start(f32[3,16,64]{2,1,0:T(8,128)S(1)} %get-tuple-element.10), channel_id=1, source_target_pairs={{1,0},{2,1},{3,2},{4,3},{5,4},{6,5},{7,6},{8,7},{9,8},{10,9},{11,1... | collective-permute-start | bytes 36872 | tf_op jit(solution)/shard_map/ppermute | solution.py:17
  14.0 110.3 %collective-permute-start.2 = (f32[3,16,64]{2,1,0:T(8,128)}, f32[3,16,64]{2,1,0:T(8,128)}, u32[]{:S(2)}, u32[]{:S(2)}) collective-permute-start(f32[3,16,64]{2,1,0:T(8,128)} %get-tuple-element.7), channel_id=1, source_target_pairs={{0,1},{1,2},{2,3},{3,4},{4,5},{5,6},{6,7},{7,8},{8,9},{9,10},{10,1... | collective-permute-start | bytes 36872 | tf_op jit(solution)/shard_map/ppermute | solution.py:16
  15.9 108.4 %collective-permute-start.3 = (f32[3,16,64]{2,1,0:T(8,128)}, f32[3,16,64]{2,1,0:T(8,128)}, u32[]{:S(2)}, u32[]{:S(2)}) collective-permute-start(f32[3,16,64]{2,1,0:T(8,128)} %get-tuple-element.8), channel_id=1, source_target_pairs={{1,0},{2,1},{3,2},{4,3},{5,4},{6,5},{7,6},{8,7},{9,8},{10,9},{11,1... | collective-permute-start | bytes 36872 | tf_op jit(solution)/shard_map/ppermute | solution.py:17
  27.4 103.4 %collective-permute-start.4 = (bf16[2,256,16]{1,2,0:T(8,128)(2,1)}, bf16[2,256,16]{1,2,0:T(8,128)(2,1)}, u32[]{:S(2)}, u32[]{:S(2)}) collective-permute-start(bf16[2,256,16]{1,2,0:T(8,128)(2,1)} %get-tuple-element.5), channel_id=1, source_target_pairs={{0,1},{1,2},{2,3},{3,4},{4,5},{5,6},{6,7},{7,8},{8,9},{9,10},{10,1... | collective-permute-start | bytes 49160 | tf_op jit(solution)/shard_map/ppermute | solution.py:16
  100.6 30.2 %collective-permute-start.5 = (bf16[2,256,16]{1,2,0:T(8,128)(2,1)}, bf16[2,256,16]{1,2,0:T(8,128)(2,1)}, u32[]{:S(2)}, u32[]{:S(2)}) collective-permute-start(bf16[2,256,16]{1,2,0:T(8,128)(2,1)} %get-tuple-element.6), channel_id=1, source_target_pairs={{1,0},{2,1},{3,2},{4,3},{5,4},{6,5},{7,6},{8,7},{9,8},{10,9},{11,1... | collective-permute-start | bytes 49160 | tf_op jit(solution)/shard_map/ppermute | solution.py:17
  117.8 12.1 %copy-start.1 = (bf16[8,256,64]{1,2,0:T(8,128)(2,1)S(1)}, bf16[8,256,64]{1,2,0:T(8,128)(2,1)}, u32[]{:S(2)}) copy-start(bf16[8,256,64]{1,2,0:T(8,128)(2,1)} %param.10) | copy-start | bytes 786436
  120.8 10.9 %copy-start.3 = (s32[1024]{0:T(1024)S(1)}, s32[1024]{0:T(1024)}, u32[]{:S(2)}) copy-start(s32[1024]{0:T(1024)} %pad_clamp_fusion) | copy-start | bytes 12292
where the time goes:
time: 136 us; the launch traced here: 135 us
  blocking collectives  60.6 us (45%)
  starting transfers between devices  41.9 us (31%)
  matrix products  18 us (13%)
  local copies, waits for them, and re-layouts  9.12 us (7%)
  other arithmetic  4.89 us (4%)
    all_gather x1, blocking collectives, body(): tops = lax.all_gather(group_total[None], 'leaf', axis=0, tiled=True)  41.4 us
    ppermute x3, starting transfers between devices, extended_2(): after = lax.ppermute(initial, axis, down)  33.6 us
    psum x1, blocking collectives, body(): group_total = lax.psum(lifted, 'grp')  19.1 us
    ppermute x3, starting transfers between devices, extended_2(): before = lax.ppermute(last, axis, up)  8.33 us
    dot_general x3, matrix products, body(): jnp.einsum('cvl,ckl->cvk', spread, transfer[0, offset:offset + clusters],...  4.37 us
    gather x2, local copies, waits for them, and re-layouts, body(): gathered = extended_levels[height][positions]  3.7 us
    dot_general x2, matrix products, body(): jnp.einsum('tcvk,tckl->tvl', gathered, couple_mat[0, offset:offset + clus...  3.53 us
    dot_general x3, matrix products, body(): jnp.einsum('cvk,ckl->cvl', coeffs[-1], transfer[0, offset:offset + cluste...  3.49 us
  transfers between devices with their start and end apart: 6, of which 0 were waited for; matrix products, arithmetic and copies ran while one was open for 19% of the time, Pallas kernels for 0%

commit v1 on v0

v1 whole, which is shorter than its diff:
```python
import functools

import jax
import jax.numpy as jnp
from jax import lax
from jax.experimental import pallas as pl
from jax.experimental.pallas import tpu as pltpu
from jax.sharding import PartitionSpec as P

MESH = pl.DeviceIdType.MESH
f32, bf16 = jnp.float32, jnp.bfloat16
NT = (((1,), (1,)), ((), ()))


def dot(a, b):
    return jnp.dot(a, b, preferred_element_type=f32)


def dot_nt(a, b):
    return lax.dot_general(a, b, NT, preferred_element_type=f32)


def parts(x):
    high = x.astype(bf16)
    return high, (x - high.astype(f32)).astype(bf16)


def twice(x):
    return jnp.concatenate([x, x], axis=1)


def kernel(
    tops, group, side,
    v_hbm, b_hbm, t_hbm, c_hbm, r_hbm, n_hbm, cs_hbm, rs_hbm, ns_hbm,
    out,
    vext, basis, transfer, couple, root, near, cs, rs, ns,
    x0, x1, lifted_rows, parts_in, tops_in, z_rows, q_high, q_low,
    in_sem, small_sem, halo_send, halo_recv, sum_send, sum_recv, top_send, top_recv, z_send, z_recv,
):
    leaf, grp = lax.axis_index("leaf"), lax.axis_index("grp")
    devices = tops * group
    me = leaf * group + grp

    def load(src, dst, sem):
        copy = pltpu.make_async_copy(src, dst, sem)
        copy.start()
        return copy

    v_copy = load(v_hbm, vext.at[pl.ds(2, 8)], in_sem.at[0])
    b_copy = load(b_hbm, basis, in_sem.at[1])
    t_copy = load(t_hbm, transfer, in_sem.at[2])
    cs_copy = load(cs_hbm, cs, small_sem.at[0])
    rs_copy = load(rs_hbm, rs, small_sem.at[1])
    ns_copy = load(ns_hbm, ns, small_sem.at[2])
    r_copy = load(r_hbm, root, in_sem.at[3])
    n_copies = [load(n_hbm.at[pl.ds(2 * i, 2)], near.at[pl.ds(2 * i, 2)], in_sem.at[5 + i]) for i in range(4)]
    c_copy = load(c_hbm, couple, in_sem.at[4])

    up, down = lax.rem(me + 1, devices), lax.rem(me + devices - 1, devices)
    up_id = (lax.div(up, group), lax.rem(up, group))
    down_id = (lax.div(down, group), lax.rem(down, group))
    barrier = pltpu.get_barrier_semaphore()

    def greet(device):
        pl.semaphore_signal(barrier, inc=1, device_id=device, device_id_type=MESH)

    def peer(o):
        return (leaf, lax.rem(grp + o, group))

    row_at, column = lax.div(leaf, side), lax.rem(leaf, side)

    def beside(o):
        return (row_at * side + lax.rem(column + o, side), grp)

    def over(o):
        return (lax.rem(row_at + o, tops // side) * side + column, grp)

    greet(up_id)
    greet(down_id)

    @pl.loop(1, group)
    def _(o):
        greet(peer(o))

    @pl.loop(1, side)
    def _(o):
        greet(beside(o))

    @pl.loop(1, tops // side)
    def _(o):
        greet(over(o))

    first = lax.broadcasted_iota(jnp.int32, (16, 128), 1) < 64
    first8 = lax.broadcasted_iota(jnp.int32, (8, 128), 1) < 64

    def split(x):
        high = x.astype(bf16).astype(f32)
        return jnp.where(first, high, x - high).astype(bf16)

    v_copy.wait()
    b_copy.wait()
    level = []
    for t in range(8):
        b = basis[t]
        x = split(dot_nt(vext[2 + t], jnp.concatenate([b, b], axis=0)))
        x0[3 + t] = x
        level.append(x)

    t_copy.wait()
    e_high, e_low = [], []
    for i in range(15):
        high, low = parts(twice(transfer[i]))
        e_high.append(high)
        e_low.append(low)

    def lift(x, i):
        weights = jnp.concatenate([e_high[i], e_high[i], e_low[i], e_low[i]], axis=0)
        return dot(twice(x), weights)

    offset = 0
    for height in range(1, 4):
        clusters = 16 >> height
        above = []
        for q in range(clusters // 2):
            x = split(lift(level[2 * q], offset + 2 * q) + lift(level[2 * q + 1], offset + 2 * q + 1))
            if height == 1:
                x1[3 + q] = x
            above.append(x)
        offset += clusters
        level = above
    top = lift(level[0], 14)
    packed = jnp.where(first8, top[0:8], top[8:16])
    lifted_rows[...] = packed.reshape(8, 1, 128)

    pl.semaphore_wait(barrier, 2 + (group - 1) + (side - 1) + (tops // side - 1))

    @pl.loop(1, group)
    def _(o):
        pltpu.make_async_remote_copy(
            lifted_rows.at[lax.rem(grp + o, group)], parts_in.at[o], sum_send, sum_recv, peer(o), MESH
        ).start()

    halos = []

    def halo(src, dst, n, device):
        copy = pltpu.make_async_remote_copy(src, dst, halo_send.at[n], halo_recv.at[n], device, MESH)
        copy.start()
        halos.append(copy)

    halo(vext.at[pl.ds(8, 2)], vext.at[pl.ds(0, 2)], 0, up_id)
    halo(vext.at[pl.ds(2, 2)], vext.at[pl.ds(10, 2)], 1, down_id)
    halo(x0.at[pl.ds(8, 3)], x0.at[pl.ds(0, 3)], 2, up_id)
    halo(x0.at[pl.ds(3, 3)], x0.at[pl.ds(11, 3)], 3, down_id)
    halo(x1.at[pl.ds(4, 3)], x1.at[pl.ds(0, 3)], 4, up_id)
    halo(x1.at[pl.ds(3, 3)], x1.at[pl.ds(7, 3)], 5, down_id)

    def chain(i, right):
        high, low = right
        e_h, e_l = e_high[i], e_low[i]
        left = jnp.where(lax.broadcasted_iota(jnp.int32, (64, 128), 1) < 64, e_h, e_l)
        return dot(twice(left), jnp.concatenate([high, high, low, low], axis=0))

    q3 = (e_high[14], e_low[14])
    q2 = [parts(chain(12 + i, q3)) for i in range(2)]
    q1 = [parts(chain(8 + i, q2[i // 2])) for i in range(4)]
    for c in range(8):
        high, low = parts(chain(c, q1[c // 2]))
        q_high[pl.ds(64 * c, 64)] = high
        q_low[pl.ds(64 * c, 64)] = low

    pltpu.make_async_copy(parts_in.at[pl.ds(1, group - 1)], parts_in.at[pl.ds(1, group - 1)], sum_recv).wait()
    total = lifted_rows[grp]
    for o in range(1, group):
        total = total + parts_in[o]
    tops_in[leaf] = total

    @pl.loop(1, side)
    def _(o):
        pltpu.make_async_remote_copy(
            tops_in.at[leaf], tops_in.at[leaf], top_send.at[0], top_recv.at[0], beside(o), MESH
        ).start()

    others = tops_in.at[pl.ds(0, side - 1)]
    pltpu.make_async_copy(others, others, top_recv.at[0]).wait()
    block = tops_in.at[pl.ds(row_at * side, side)]

    @pl.loop(1, tops // side)
    def _(o):
        pltpu.make_async_remote_copy(block, block, top_send.at[1], top_recv.at[1], over(o), MESH).start()

    r_copy.wait()
    diagonal = []
    for j in range(4):
        m = root[j]
        zero = jnp.zeros_like(m)
        diagonal.append(
            parts(jnp.concatenate([jnp.concatenate([m, zero], axis=1), jnp.concatenate([zero, m], axis=1)], axis=0))
        )
    rs_copy.wait()
    ns_copy.wait()
    cs_copy.wait()
    for copy in halos:
        copy.wait_recv()
    for copy in n_copies:
        copy.wait()
    for t in range(8):
        total = dot_nt(vext[2 + t], near[t, 0])
        for e in range(1, 3):
            place = jnp.minimum(jnp.bitwise_and(ns[e, t] - 8 * me + 2, 8 * devices - 1), 11)
            total = total + dot_nt(vext[place], near[t, e])
        out[t] = total

    c_copy.wait()

    def coupling(x, row, base, cycle):
        total = None
        for j in range(3):
            place = jnp.minimum(jnp.bitwise_and(cs[j, 0, row] - base + 3, cycle - 1), x.shape[0] - 1)
            high, low = parts(couple[3 * row + j])
            term = dot(twice(x[place]), jnp.concatenate([high, high, low, low], axis=0))
            total = term if total is None else total + term
        return total

    pairs = []
    for q in range(4):
        y1 = split(twice(coupling(x1, 8 + q, 4 * me, 4 * devices)))
        weights = jnp.concatenate(
            [
                jnp.concatenate([e_high[2 * q], e_low[2 * q]], axis=1),
                jnp.concatenate([e_high[2 * q + 1], e_low[2 * q + 1]], axis=1),
            ],
            axis=0,
        )
        y0 = [coupling(x0, 2 * q + i, 8 * me, 8 * devices) for i in range(2)]
        pairs.append(dot_nt(twice(y1), weights) + jnp.concatenate(y0, axis=1))
    base = jnp.concatenate(pairs, axis=1)

    others = tops_in.at[pl.ds(0, tops - side)]
    pltpu.make_async_copy(others, others, top_recv.at[1]).wait()
    row = None
    for j in range(4):
        slot = jnp.bitwise_and(rs[0, j], tops - 1)
        g_high, g_low = parts(tops_in[slot])
        r_high, r_low = diagonal[j]
        term = dot(g_high, r_high) + dot(g_low, r_high) + dot(g_high, r_low)
        row = term if row is None else row + term
    z_rows[grp] = row

    @pl.loop(1, group)
    def _(o):
        pltpu.make_async_remote_copy(z_rows.at[grp], z_rows.at[grp], z_send, z_recv.at[grp], peer(o), MESH).start()

    @pl.loop(1, group)
    def _(o):
        other = lax.rem(grp + o, group)
        pltpu.make_async_remote_copy(
            z_rows.at[other], z_rows.at[other], z_send, z_recv.at[other], peer(o), MESH
        ).wait_recv()

    z = z_rows[...].reshape(8, 128)
    zero = jnp.zeros_like(z)
    z = jnp.concatenate([jnp.where(first8, z, zero), jnp.where(first8, zero, z)], axis=0)
    z_high, z_low = parts(z)
    low_q = q_low[...]
    high_q = q_high[...]
    w = dot_nt(z_high, high_q) + dot_nt(z_low, high_q) + dot_nt(z_high, low_q) + base
    w = w.astype(bf16)
    nothing = jnp.zeros((16, 128), bf16)
    for q in range(4):
        pair = w[:, 128 * q : 128 * (q + 1)]
        left = jnp.concatenate([jnp.where(first, pair, nothing), jnp.where(first, nothing, pair)], axis=0)
        product = dot(left, basis[2 * q : 2 * q + 2].reshape(128, 256))
        out[2 * q] = out[2 * q] + product[0:16]
        out[2 * q + 1] = out[2 * q + 1] + product[16:32]

    for copy in halos:
        copy.wait_send()
    sent = parts_in.at[pl.ds(1, group - 1)]
    pltpu.make_async_copy(sent, sent, sum_send).wait()
    pltpu.make_async_copy(sent, sent, z_send).wait()
    sent = tops_in.at[pl.ds(0, side - 1)]
    pltpu.make_async_copy(sent, sent, top_send.at[0]).wait()
    sent = tops_in.at[pl.ds(0, tops - side)]
    pltpu.make_async_copy(sent, sent, top_send.at[1]).wait()


def solution(mesh):
    tops, group = mesh.shape["leaf"], mesh.shape["grp"]

    def body(vectors, leaf_basis, transfer, couple_src, couple_mat, root_src, root_mat, near_src, near_blocks):
        args = (
            vectors.transpose(0, 2, 1),
            leaf_basis.transpose(0, 2, 1),
            transfer.reshape(15, 64, 64),
            couple_mat.reshape(36, 64, 64),
            root_mat.reshape(4, 64, 64),
            near_blocks.transpose(0, 2, 1, 3),
            couple_src.transpose(2, 0, 1),
            root_src,
            near_src.transpose(1, 0),
        )
        hbm = pl.BlockSpec(memory_space=pltpu.HBM)
        dma = pltpu.SemaphoreType.DMA
        result = pl.pallas_call(
            functools.partial(kernel, tops, group, 8),
            out_shape=pltpu.VMEM((8, 16, 256), f32),
            in_specs=[hbm] * 9,
            out_specs=pl.BlockSpec(memory_space=pltpu.VMEM),
            scratch_shapes=[
                pltpu.VMEM((12, 16, 256), bf16),
                pltpu.VMEM((8, 64, 256), bf16),
                pltpu.VMEM((15, 64, 64), f32),
                pltpu.VMEM((36, 64, 64), f32),
                pltpu.VMEM((4, 64, 64), f32),
                pltpu.VMEM((8, 3, 256, 256), bf16),
                pltpu.SMEM((3, 1, 12), jnp.int32),
                pltpu.SMEM((1, 4), jnp.int32),
                pltpu.SMEM((3, 8), jnp.int32),
                pltpu.VMEM((14, 16, 128), bf16),
                pltpu.VMEM((10, 16, 128), bf16),
                pltpu.VMEM((8, 1, 128), f32),
                pltpu.VMEM((8, 1, 128), f32),
                pltpu.VMEM((tops, 1, 128), f32),
                pltpu.VMEM((8, 1, 128), f32),
                pltpu.VMEM((512, 128), bf16),
                pltpu.VMEM((512, 128), bf16),
                dma((9,)),
                dma((3,)),
                dma((6,)),
                dma((6,)),
                dma,
                dma,
                dma((2,)),
                dma((2,)),
                dma,
                dma((8,)),
            ],
            compiler_params=pltpu.CompilerParams(
                collective_id=0, has_side_effects=True, vmem_limit_bytes=32 * 1024 * 1024
            ),
            name="h2",
        )(*(pltpu.with_memory_space_constraint(a, pltpu.HBM) for a in args))
        return result.transpose(0, 2, 1)

    both = ("leaf", "grp")
    in_specs = (
        P(both, None, None),
        P(both, None, None),
        P(both, None, None, None),
        P(both, None, None),
        P(both, None, None, None, None),
        P("leaf", None),
        P("leaf", None, None, None),
        P(both, None),
        P(both, None, None, None),
    )
    return jax.shard_map(body, mesh=mesh, in_specs=in_specs, out_specs=P(both, None, None), check_vma=False)
```

time: 136 us -> 32.3 us (0.24)
  blocking collectives: 60.6 us -> 0 us
  starting transfers between devices: 41.9 us -> 0 us
  Pallas kernels: 0 us -> 31.6 us
  matrix products: 18 us -> 0 us
  local copies, waits for them, and re-layouts: 9.12 us -> 0.66 us
  other arithmetic: 4.89 us -> 0 us
    ppermute x6 -> x0, starting transfers between devices: 41.9 us -> none  [the longest x3 33.6 us: extended_2(): after = lax.ppermute(initial, axis, down)]
    all_gather x1 -> x0, blocking collectives: 41.4 us -> none  [body(): tops = lax.all_gather(group_total[None], 'leaf', axis=0, tiled=True)]
    pallas_call x0 -> x1, Pallas kernels: none -> 31.6 us  [body(): pl.pallas_call(functools.partial(kernel, tops, group, 8), out_shape=pltpu...]
    psum x1 -> x0, blocking collectives: 19.1 us -> none  [body(): group_total = lax.psum(lifted, 'grp')]
    dot_general x14 -> x0, matrix products: 18 us -> none  [the longest x3 4.37 us: body(): jnp.einsum('cvl,ckl->cvk', spread, transfer[0, offset:offset + clusters],...]
    gather x4 -> x0, local copies, waits for them, and re-layouts: 5.85 us -> none  [the longest x2 3.7 us: body(): gathered = extended_levels[height][positions]]
    concatenate x3 -> x0, other arithmetic: 2.3 us -> none  [extended_2(): array = jnp.concatenate([before, array, after], axis=dim)]
    slice x3 -> x0, local copies, waits for them, and re-layouts: 1.97 us -> none  [extended_2(): last = lax.slice_in_dim(array, length - width, length, axis=dim)]
  transfers between devices with their start and end apart: 6 -> 0, of which waited for: 0 -> 0; matrix products, arithmetic and copies ran while one was open for 19% -> 0% of each run, Pallas kernels for 0% -> 0%
where the time goes in v1:
time: 32.3 us; the launch traced here: 32.2 us
  Pallas kernels  31.6 us (98%)
  local copies, waits for them, and re-layouts  0.66 us (2%)
    pallas_call x1, Pallas kernels, body(): pl.pallas_call(functools.partial(kernel, tops, group, 8), out_shape=pltpu...  31.6 us
    unnamed x1, local copies, waits for them, and re-layouts  0.66 us

profile of v1, /device:TPU:1, one launch (start us, length us, event | category | flops | bytes accessed | tf_op | source)
XLA Modules:
  0.0 32.2 jit_solution(3658144609977473372)
XLA Ops:
  0.0 31.6 %h2.1 = f32[8,16,256]{2,1,0:T(8,128)S(1)} custom-call(bf16[8,16,256]{2,1,0:T(8,128)(2,1)} %bitcast.15, bf16[8,64,256]{2,1,0:T(8,128)(2,1)} %bitcast.13, f32[15,64,64]{2,1,0:T(8,128)} %bitcast.12, f32[36,64,64]{2,1,0:T(8,128)} %bitcast.11, f32[4,64,64]{2,1,0:T(8,128)} %bitcast.14, bf16[8,3,256,256]{3,2,1,0:T(8,128)(2,1)} %bitcast.10, s32[3,1,12]{2,1,0:T(1,128)} %bitcast.17, ...), custom_call_target="tpu_custom_call" | custom-call | tf_op jit(solution)/shard_map/h2/pallas_call | solution.py:304
  31.6 0.7 %copy.11 = f32[8,256,16]{1,2,0:T(8,128)} copy(f32[8,256,16]{1,2,0:T(8,128)S(1)} %bitcast.9) | data formatting | bytes 262144

commit v2 on v1

--- a/solution.py
+++ b/solution.py
@@ -9,6 +9,7 @@
 
 MESH = pl.DeviceIdType.MESH
 f32, bf16 = jnp.float32, jnp.bfloat16
+RELAY = 5
 NT = (((1,), (1,)), ((), ()))
 
 
@@ -34,8 +35,8 @@
     v_hbm, b_hbm, t_hbm, c_hbm, r_hbm, n_hbm, cs_hbm, rs_hbm, ns_hbm,
     out,
     vext, basis, transfer, couple, root, near, cs, rs, ns,
-    x0, x1, lifted_rows, parts_in, tops_in, z_rows, q_high, q_low,
-    in_sem, small_sem, halo_send, halo_recv, sum_send, sum_recv, top_send, top_recv, z_send, z_recv,
+    x0, x1, lifted_rows, parts_in, tops_in, z_rows, q_high, q_low, stack,
+    in_sem, small_sem, halo_send, halo_recv, sum_send, sum_recv, own_send, relay_send, top_recv, z_send, z_recv,
 ):
     leaf, grp = lax.axis_index("leaf"), lax.axis_index("grp")
     devices = tops * group
@@ -52,9 +53,6 @@
     cs_copy = load(cs_hbm, cs, small_sem.at[0])
     rs_copy = load(rs_hbm, rs, small_sem.at[1])
     ns_copy = load(ns_hbm, ns, small_sem.at[2])
-    r_copy = load(r_hbm, root, in_sem.at[3])
-    n_copies = [load(n_hbm.at[pl.ds(2 * i, 2)], near.at[pl.ds(2 * i, 2)], in_sem.at[5 + i]) for i in range(4)]
-    c_copy = load(c_hbm, couple, in_sem.at[4])
 
     up, down = lax.rem(me + 1, devices), lax.rem(me + devices - 1, devices)
     up_id = (lax.div(up, group), lax.rem(up, group))
@@ -64,31 +62,44 @@
     def greet(device):
         pl.semaphore_signal(barrier, inc=1, device_id=device, device_id_type=MESH)
 
+    def turn(i, n):
+        return jnp.where(i >= n, i - n, i)
+
     def peer(o):
-        return (leaf, lax.rem(grp + o, group))
+        return (leaf, turn(grp + o, group))
 
     row_at, column = lax.div(leaf, side), lax.rem(leaf, side)
-
-    def beside(o):
-        return (row_at * side + lax.rem(column + o, side), grp)
-
-    def over(o):
-        return (lax.rem(row_at + o, tops // side) * side + column, grp)
+    planes = tops // side
+    plane = side * group
+    place_in = column * group + grp
+
+    def at(z):
+        return (z * side + column, grp)
+
+    def sends(z, t):
+        return (z != t) & ((t <= RELAY) | ((z != RELAY - 1) & (z != RELAY - 2)))
+
+    is_relayed = (row_at == RELAY - 1) | (row_at == RELAY - 2)
+    targets = planes - 1 - jnp.where(is_relayed, planes - 1 - RELAY, 0)
+
+    def through_plane(act):
+        @pl.loop(0, side - 1)
+        def _(k):
+            o = turn(k + side // 2, side)
+            other = row_at * side + turn(column + jnp.where(k + side // 2 >= side, o + 1, o), side)
+            for g in range(group):
+                act((other, g), g)
+
+        for o in range(1, group):
+            device = peer(o)
+            act(device, device[1])
 
     greet(up_id)
     greet(down_id)
-
-    @pl.loop(1, group)
-    def _(o):
-        greet(peer(o))
-
-    @pl.loop(1, side)
-    def _(o):
-        greet(beside(o))
-
-    @pl.loop(1, tops // side)
-    def _(o):
-        greet(over(o))
+    through_plane(lambda device, g: greet(device))
+
+    for z in range(planes):
+        pl.when(sends(z, row_at))(functools.partial(lambda z: greet(at(z)), z))
 
     first = lax.broadcasted_iota(jnp.int32, (16, 128), 1) < 64
     first8 = lax.broadcasted_iota(jnp.int32, (8, 128), 1) < 64
@@ -107,6 +118,9 @@
         level.append(x)
 
     t_copy.wait()
+    r_copy = load(r_hbm, root, in_sem.at[3])
+    n_copies = [load(n_hbm.at[pl.ds(2 * i, 2)], near.at[pl.ds(2 * i, 2)], in_sem.at[5 + i]) for i in range(4)]
+    c_copy = load(c_hbm, couple, in_sem.at[4])
     e_high, e_low = [], []
     for i in range(15):
         high, low = parts(twice(transfer[i]))
@@ -132,13 +146,15 @@
     packed = jnp.where(first8, top[0:8], top[8:16])
     lifted_rows[...] = packed.reshape(8, 1, 128)
 
-    pl.semaphore_wait(barrier, 2 + (group - 1) + (side - 1) + (tops // side - 1))
-
-    @pl.loop(1, group)
-    def _(o):
+    pl.semaphore_wait(barrier, 2 + (plane - 1) + targets)
+
+    def hand_out(device, g):
         pltpu.make_async_remote_copy(
-            lifted_rows.at[lax.rem(grp + o, group)], parts_in.at[o], sum_send, sum_recv, peer(o), MESH
+            lifted_rows.at[g], parts_in.at[place_in], sum_send, sum_recv, device, MESH
         ).start()
+
+    through_plane(hand_out)
+    parts_in[place_in] = lifted_rows[grp]
 
     halos = []
 
@@ -168,43 +184,55 @@
         q_high[pl.ds(64 * c, 64)] = high
         q_low[pl.ds(64 * c, 64)] = low
 
-    pltpu.make_async_copy(parts_in.at[pl.ds(1, group - 1)], parts_in.at[pl.ds(1, group - 1)], sum_recv).wait()
-    total = lifted_rows[grp]
-    for o in range(1, group):
-        total = total + parts_in[o]
-    tops_in[leaf] = total
-
-    @pl.loop(1, side)
-    def _(o):
-        pltpu.make_async_remote_copy(
-            tops_in.at[leaf], tops_in.at[leaf], top_send.at[0], top_recv.at[0], beside(o), MESH
-        ).start()
-
-    others = tops_in.at[pl.ds(0, side - 1)]
-    pltpu.make_async_copy(others, others, top_recv.at[0]).wait()
-    block = tops_in.at[pl.ds(row_at * side, side)]
-
-    @pl.loop(1, tops // side)
-    def _(o):
-        pltpu.make_async_remote_copy(block, block, top_send.at[1], top_recv.at[1], over(o), MESH).start()
-
     r_copy.wait()
-    diagonal = []
+    highs, lows = [], []
     for j in range(4):
         m = root[j]
         zero = jnp.zeros_like(m)
-        diagonal.append(
-            parts(jnp.concatenate([jnp.concatenate([m, zero], axis=1), jnp.concatenate([zero, m], axis=1)], axis=0))
-        )
+        diagonal = jnp.concatenate([jnp.concatenate([m, zero], axis=1), jnp.concatenate([zero, m], axis=1)], axis=0)
+        high, low = parts(diagonal)
+        highs.append(high)
+        lows.append(low)
+    stack[...] = jnp.concatenate(highs + highs + lows, axis=0)
+    for i in range(4):
+        n_copies[i].wait()
+        for t in range(2 * i, 2 * i + 2):
+            out[t] = dot_nt(vext[2 + t], near[t, 0])
+
+    others = parts_in.at[pl.ds(0, plane - 1)]
+    pltpu.make_async_copy(others, others, sum_recv).wait()
+    sums = parts_in[...].reshape(side, group, 128).sum(axis=1)
+    tops_in[pl.ds(row_at * side, side)] = sums.reshape(side, 1, 128)
+
+    def block(z):
+        return tops_in.at[pl.ds(z * side, side)]
+
+    def pass_on(z, send, target):
+        return pltpu.make_async_remote_copy(block(z), block(z), send, top_recv.at[z], at(target), MESH)
+
+    def arrive(z):
+        pltpu.make_async_copy(block(z), block(z), top_recv.at[z]).wait()
+
+    def each_target(act):
+        for z in range(planes):
+            pl.when(sends(row_at, z))(functools.partial(act, z))
+
+    each_target(lambda z: pass_on(row_at, own_send.at[z], z).start())
+
+    @pl.when(row_at == RELAY)
+    def _():
+        for i in range(2):
+            arrive(RELAY - 1 - i)
+            for z in range(RELAY + 1, planes):
+                pass_on(RELAY - 1 - i, relay_send.at[i, z], z).start()
+
     rs_copy.wait()
     ns_copy.wait()
     cs_copy.wait()
     for copy in halos:
         copy.wait_recv()
-    for copy in n_copies:
-        copy.wait()
     for t in range(8):
-        total = dot_nt(vext[2 + t], near[t, 0])
+        total = out[t]
         for e in range(1, 3):
             place = jnp.minimum(jnp.bitwise_and(ns[e, t] - 8 * me + 2, 8 * devices - 1), 11)
             total = total + dot_nt(vext[place], near[t, e])
@@ -235,27 +263,21 @@
         pairs.append(dot_nt(twice(y1), weights) + jnp.concatenate(y0, axis=1))
     base = jnp.concatenate(pairs, axis=1)
 
-    others = tops_in.at[pl.ds(0, tops - side)]
-    pltpu.make_async_copy(others, others, top_recv.at[1]).wait()
-    row = None
-    for j in range(4):
-        slot = jnp.bitwise_and(rs[0, j], tops - 1)
-        g_high, g_low = parts(tops_in[slot])
-        r_high, r_low = diagonal[j]
-        term = dot(g_high, r_high) + dot(g_low, r_high) + dot(g_high, r_low)
-        row = term if row is None else row + term
+    for z in range(planes):
+        expected = row_at != z
+        if z in (RELAY - 1, RELAY - 2):
+            expected = expected & (row_at != RELAY)
+        pl.when(expected)(functools.partial(arrive, z))
+
+    g = jnp.concatenate([tops_in[jnp.bitwise_and(rs[0, j], tops - 1)] for j in range(4)], axis=1)
+    high, low = parts(g)
+    row = dot(jnp.concatenate([high, low, high], axis=1), stack[...])
     z_rows[grp] = row
 
-    @pl.loop(1, group)
-    def _(o):
-        pltpu.make_async_remote_copy(z_rows.at[grp], z_rows.at[grp], z_send, z_recv.at[grp], peer(o), MESH).start()
-
-    @pl.loop(1, group)
-    def _(o):
-        other = lax.rem(grp + o, group)
-        pltpu.make_async_remote_copy(
-            z_rows.at[other], z_rows.at[other], z_send, z_recv.at[other], peer(o), MESH
-        ).wait_recv()
+    for o in range(1, group):
+        pltpu.make_async_remote_copy(z_rows.at[grp], z_rows.at[grp], z_send, z_recv, peer(o), MESH).start()
+    others = z_rows.at[pl.ds(0, group - 1)]
+    pltpu.make_async_copy(others, others, z_recv).wait()
 
     z = z_rows[...].reshape(8, 128)
     zero = jnp.zeros_like(z)
@@ -263,7 +285,8 @@
     z_high, z_low = parts(z)
     low_q = q_low[...]
     high_q = q_high[...]
-    w = dot_nt(z_high, high_q) + dot_nt(z_low, high_q) + dot_nt(z_high, low_q) + base
+    product = dot_nt(jnp.concatenate([z_high, z_low], axis=0), high_q)
+    w = product[0:16] + product[16:32] + dot_nt(z_high, low_q) + base
     w = w.astype(bf16)
     nothing = jnp.zeros((16, 128), bf16)
     for q in range(4):
@@ -275,13 +298,19 @@
 
     for copy in halos:
         copy.wait_send()
-    sent = parts_in.at[pl.ds(1, group - 1)]
+    sent = parts_in.at[pl.ds(0, plane - 1)]
     pltpu.make_async_copy(sent, sent, sum_send).wait()
+
+    each_target(lambda z: pass_on(row_at, own_send.at[z], z).wait_send())
+
+    @pl.when(row_at == RELAY)
+    def _():
+        for i in range(2):
+            for z in range(RELAY + 1, planes):
+                pass_on(RELAY - 1 - i, relay_send.at[i, z], z).wait_send()
+
+    sent = parts_in.at[pl.ds(0, group - 1)]
     pltpu.make_async_copy(sent, sent, z_send).wait()
-    sent = tops_in.at[pl.ds(0, side - 1)]
-    pltpu.make_async_copy(sent, sent, top_send.at[0]).wait()
-    sent = tops_in.at[pl.ds(0, tops - side)]
-    pltpu.make_async_copy(sent, sent, top_send.at[1]).wait()
 
 
 def solution(mesh):
@@ -319,21 +348,23 @@
                 pltpu.VMEM((14, 16, 128), bf16),
                 pltpu.VMEM((10, 16, 128), bf16),
                 pltpu.VMEM((8, 1, 128), f32),
-                pltpu.VMEM((8, 1, 128), f32),
+                pltpu.VMEM((64, 1, 128), f32),
                 pltpu.VMEM((tops, 1, 128), f32),
                 pltpu.VMEM((8, 1, 128), f32),
                 pltpu.VMEM((512, 128), bf16),
                 pltpu.VMEM((512, 128), bf16),
+                pltpu.VMEM((1536, 128), bf16),
                 dma((9,)),
                 dma((3,)),
                 dma((6,)),
                 dma((6,)),
                 dma,
                 dma,
-                dma((2,)),
-                dma((2,)),
+                dma((8,)),
+                dma((2, 8)),
+                dma((8,)),
                 dma,
-                dma((8,)),
+                dma,
             ],
             compiler_params=pltpu.CompilerParams(
                 collective_id=0, has_side_effects=True, vmem_limit_bytes=32 * 1024 * 1024

time: 32.3 us -> 29.6 us (0.916)
  Pallas kernels: 31.6 us -> 28.8 us
    pallas_call x1, Pallas kernels: 31.6 us -> 28.8 us  [body(): pl.pallas_call(functools.partial(kernel, tops, group, 8), out_shape=pltpu...]
where the time goes in v2:
time: 29.6 us; the launch traced here: 29.5 us
  Pallas kernels  28.8 us (97%)
  local copies, waits for them, and re-layouts  0.66 us (2%)
    pallas_call x1, Pallas kernels, body(): pl.pallas_call(functools.partial(kernel, tops, group, 8), out_shape=pltpu...  28.8 us
    unnamed x1, local copies, waits for them, and re-layouts  0.66 us

profile of v2, /device:TPU:1, one launch (start us, length us, event | category | flops | bytes accessed | tf_op | source)
XLA Modules:
  0.0 29.5 jit_solution(7312503398339767389)
XLA Ops:
  0.0 28.8 %h2.1 = f32[8,16,256]{2,1,0:T(8,128)S(1)} custom-call(bf16[8,16,256]{2,1,0:T(8,128)(2,1)} %bitcast.15, bf16[8,64,256]{2,1,0:T(8,128)(2,1)} %bitcast.13, f32[15,64,64]{2,1,0:T(8,128)} %bitcast.12, f32[36,64,64]{2,1,0:T(8,128)} %bitcast.11, f32[4,64,64]{2,1,0:T(8,128)} %bitcast.14, bf16[8,3,256,256]{3,2,1,0:T(8,128)(2,1)} %bitcast.10, s32[3,1,12]{2,1,0:T(1,128)} %bitcast.17, ...), custom_call_target="tpu_custom_call" | custom-call | tf_op jit(solution)/shard_map/h2/pallas_call | solution.py:333
  28.8 0.7 %copy.11 = f32[8,256,16]{1,2,0:T(8,128)} copy(f32[8,256,16]{1,2,0:T(8,128)S(1)} %bitcast.9) | data formatting | bytes 262144

commit v3 on v2

--- a/solution.py
+++ b/solution.py
@@ -10,6 +10,7 @@
 MESH = pl.DeviceIdType.MESH
 f32, bf16 = jnp.float32, jnp.bfloat16
 RELAY = 5
+OWNERS = 4
 NT = (((1,), (1,)), ((), ()))
 
 
@@ -50,9 +51,6 @@
     v_copy = load(v_hbm, vext.at[pl.ds(2, 8)], in_sem.at[0])
     b_copy = load(b_hbm, basis, in_sem.at[1])
     t_copy = load(t_hbm, transfer, in_sem.at[2])
-    cs_copy = load(cs_hbm, cs, small_sem.at[0])
-    rs_copy = load(rs_hbm, rs, small_sem.at[1])
-    ns_copy = load(ns_hbm, ns, small_sem.at[2])
 
     up, down = lax.rem(me + 1, devices), lax.rem(me + devices - 1, devices)
     up_id = (lax.div(up, group), lax.rem(up, group))
@@ -82,24 +80,35 @@
     is_relayed = (row_at == RELAY - 1) | (row_at == RELAY - 2)
     targets = planes - 1 - jnp.where(is_relayed, planes - 1 - RELAY, 0)
 
-    def through_plane(act):
+    owner = grp < OWNERS
+
+    def through_columns(act, count):
         @pl.loop(0, side - 1)
         def _(k):
             o = turn(k + side // 2, side)
             other = row_at * side + turn(column + jnp.where(k + side // 2 >= side, o + 1, o), side)
-            for g in range(group):
+            for g in range(count):
                 act((other, g), g)
 
+    def owners_here(act):
+        for g in range(OWNERS):
+            pl.when(grp != g)(functools.partial(act, (leaf, g), g))
+
+    @pl.when(owner)
+    def _():
+        through_columns(lambda device, g: greet(device), group)
         for o in range(1, group):
-            device = peer(o)
-            act(device, device[1])
+            greet(peer(o))
+        for z in range(planes):
+            pl.when(sends(z, row_at))(functools.partial(lambda z: greet(at(z)), z))
+
+    @pl.when(grp >= OWNERS)
+    def _():
+        for g in range(OWNERS):
+            greet((leaf, g))
 
     greet(up_id)
     greet(down_id)
-    through_plane(lambda device, g: greet(device))
-
-    for z in range(planes):
-        pl.when(sends(z, row_at))(functools.partial(lambda z: greet(at(z)), z))
 
     first = lax.broadcasted_iota(jnp.int32, (16, 128), 1) < 64
     first8 = lax.broadcasted_iota(jnp.int32, (8, 128), 1) < 64
@@ -118,6 +127,9 @@
         level.append(x)
 
     t_copy.wait()
+    cs_copy = load(cs_hbm, cs, small_sem.at[0])
+    rs_copy = load(rs_hbm, rs, small_sem.at[1])
+    ns_copy = load(ns_hbm, ns, small_sem.at[2])
     r_copy = load(r_hbm, root, in_sem.at[3])
     n_copies = [load(n_hbm.at[pl.ds(2 * i, 2)], near.at[pl.ds(2 * i, 2)], in_sem.at[5 + i]) for i in range(4)]
     c_copy = load(c_hbm, couple, in_sem.at[4])
@@ -131,8 +143,15 @@
         weights = jnp.concatenate([e_high[i], e_high[i], e_low[i], e_low[i]], axis=0)
         return dot(twice(x), weights)
 
+    def chain(i, right):
+        high, low = right
+        e_h, e_l = e_high[i], e_low[i]
+        left = jnp.where(lax.broadcasted_iota(jnp.int32, (64, 128), 1) < 64, e_h, e_l)
+        return dot(twice(left), jnp.concatenate([high, high, low, low], axis=0))
+
+    q2 = [parts(chain(12 + i, (e_high[14], e_low[14]))) for i in range(2)]
     offset = 0
-    for height in range(1, 4):
+    for height in range(1, 3):
         clusters = 16 >> height
         above = []
         for q in range(clusters // 2):
@@ -142,19 +161,29 @@
             above.append(x)
         offset += clusters
         level = above
-    top = lift(level[0], 14)
+    top = None
+    for x, (high, low) in zip(level, q2):
+        term = dot(twice(x), jnp.concatenate([high, high, low, low], axis=0))
+        top = term if top is None else top + term
     packed = jnp.where(first8, top[0:8], top[8:16])
-    lifted_rows[...] = packed.reshape(8, 1, 128)
-
-    pl.semaphore_wait(barrier, 2 + (plane - 1) + targets)
+    for i in range(4):
+        lifted_rows[i] = packed[2 * i : 2 * i + 2]
+
+    pl.semaphore_wait(
+        barrier, 2 + side * OWNERS + jnp.where(owner, group - OWNERS - 1 + targets, 0)
+    )
 
     def hand_out(device, g):
         pltpu.make_async_remote_copy(
             lifted_rows.at[g], parts_in.at[place_in], sum_send, sum_recv, device, MESH
         ).start()
 
-    through_plane(hand_out)
-    parts_in[place_in] = lifted_rows[grp]
+    through_columns(hand_out, OWNERS)
+    owners_here(hand_out)
+
+    @pl.when(owner)
+    def _():
+        parts_in[place_in] = lifted_rows[grp]
 
     halos = []
 
@@ -170,14 +199,6 @@
     halo(x1.at[pl.ds(4, 3)], x1.at[pl.ds(0, 3)], 4, up_id)
     halo(x1.at[pl.ds(3, 3)], x1.at[pl.ds(7, 3)], 5, down_id)
 
-    def chain(i, right):
-        high, low = right
-        e_h, e_l = e_high[i], e_low[i]
-        left = jnp.where(lax.broadcasted_iota(jnp.int32, (64, 128), 1) < 64, e_h, e_l)
-        return dot(twice(left), jnp.concatenate([high, high, low, low], axis=0))
-
-    q3 = (e_high[14], e_low[14])
-    q2 = [parts(chain(12 + i, q3)) for i in range(2)]
     q1 = [parts(chain(8 + i, q2[i // 2])) for i in range(4)]
     for c in range(8):
         high, low = parts(chain(c, q1[c // 2]))
@@ -199,11 +220,6 @@
         for t in range(2 * i, 2 * i + 2):
             out[t] = dot_nt(vext[2 + t], near[t, 0])
 
-    others = parts_in.at[pl.ds(0, plane - 1)]
-    pltpu.make_async_copy(others, others, sum_recv).wait()
-    sums = parts_in[...].reshape(side, group, 128).sum(axis=1)
-    tops_in[pl.ds(row_at * side, side)] = sums.reshape(side, 1, 128)
-
     def block(z):
         return tops_in.at[pl.ds(z * side, side)]
 
@@ -217,9 +233,14 @@
         for z in range(planes):
             pl.when(sends(row_at, z))(functools.partial(act, z))
 
-    each_target(lambda z: pass_on(row_at, own_send.at[z], z).start())
-
-    @pl.when(row_at == RELAY)
+    @pl.when(owner)
+    def _():
+        others = parts_in.at[pl.ds(0, plane - 1)]
+        pltpu.make_async_copy(others, others, sum_recv).wait()
+        tops_in[pl.ds(row_at * side, side)] = parts_in[...].reshape(side, group, 2, 128).sum(axis=1)
+        each_target(lambda z: pass_on(row_at, own_send.at[z], z).start())
+
+    @pl.when(owner & (row_at == RELAY))
     def _():
         for i in range(2):
             arrive(RELAY - 1 - i)
@@ -263,23 +284,26 @@
         pairs.append(dot_nt(twice(y1), weights) + jnp.concatenate(y0, axis=1))
     base = jnp.concatenate(pairs, axis=1)
 
-    for z in range(planes):
-        expected = row_at != z
-        if z in (RELAY - 1, RELAY - 2):
-            expected = expected & (row_at != RELAY)
-        pl.when(expected)(functools.partial(arrive, z))
-
-    g = jnp.concatenate([tops_in[jnp.bitwise_and(rs[0, j], tops - 1)] for j in range(4)], axis=1)
-    high, low = parts(g)
-    row = dot(jnp.concatenate([high, low, high], axis=1), stack[...])
-    z_rows[grp] = row
-
-    for o in range(1, group):
-        pltpu.make_async_remote_copy(z_rows.at[grp], z_rows.at[grp], z_send, z_recv, peer(o), MESH).start()
-    others = z_rows.at[pl.ds(0, group - 1)]
-    pltpu.make_async_copy(others, others, z_recv).wait()
-
-    z = z_rows[...].reshape(8, 128)
+    @pl.when(owner)
+    def _():
+        for z in range(planes):
+            expected = row_at != z
+            if z in (RELAY - 1, RELAY - 2):
+                expected = expected & (row_at != RELAY)
+            pl.when(expected)(functools.partial(arrive, z))
+        g = jnp.concatenate([tops_in[jnp.bitwise_and(rs[0, j], tops - 1)] for j in range(4)], axis=1)
+        high, low = parts(g)
+        z_rows[grp] = dot(jnp.concatenate([high, low, high], axis=1), stack[...])
+        for o in range(1, group):
+            pltpu.make_async_remote_copy(z_rows.at[grp], z_rows.at[grp], z_send, z_recv, peer(o), MESH).start()
+        others = z_rows.at[pl.ds(0, OWNERS - 1)]
+        pltpu.make_async_copy(others, others, z_recv).wait()
+
+    @pl.when(grp >= OWNERS)
+    def _():
+        pltpu.make_async_copy(z_rows, z_rows, z_recv).wait()
+
+    z = jnp.concatenate([z_rows[i] for i in range(4)], axis=0)
     zero = jnp.zeros_like(z)
     z = jnp.concatenate([jnp.where(first8, z, zero), jnp.where(first8, zero, z)], axis=0)
     z_high, z_low = parts(z)
@@ -298,19 +322,25 @@
 
     for copy in halos:
         copy.wait_send()
-    sent = parts_in.at[pl.ds(0, plane - 1)]
-    pltpu.make_async_copy(sent, sent, sum_send).wait()
-
-    each_target(lambda z: pass_on(row_at, own_send.at[z], z).wait_send())
-
-    @pl.when(row_at == RELAY)
+
+    @pl.when(owner)
+    def _():
+        sent = parts_in.at[pl.ds(0, side * OWNERS - 1)]
+        pltpu.make_async_copy(sent, sent, sum_send).wait()
+        each_target(lambda z: pass_on(row_at, own_send.at[z], z).wait_send())
+        rows = parts_in.at[pl.ds(0, group - 1)]
+        pltpu.make_async_copy(rows, rows, z_send).wait()
+
+    @pl.when(grp >= OWNERS)
+    def _():
+        sent = parts_in.at[pl.ds(0, side * OWNERS)]
+        pltpu.make_async_copy(sent, sent, sum_send).wait()
+
+    @pl.when(owner & (row_at == RELAY))
     def _():
         for i in range(2):
             for z in range(RELAY + 1, planes):
                 pass_on(RELAY - 1 - i, relay_send.at[i, z], z).wait_send()
-
-    sent = parts_in.at[pl.ds(0, group - 1)]
-    pltpu.make_async_copy(sent, sent, z_send).wait()
 
 
 def solution(mesh):
@@ -347,10 +377,10 @@
                 pltpu.SMEM((3, 8), jnp.int32),
                 pltpu.VMEM((14, 16, 128), bf16),
                 pltpu.VMEM((10, 16, 128), bf16),
-                pltpu.VMEM((8, 1, 128), f32),
-                pltpu.VMEM((64, 1, 128), f32),
-                pltpu.VMEM((tops, 1, 128), f32),
-                pltpu.VMEM((8, 1, 128), f32),
+                pltpu.VMEM((4, 2, 128), f32),
+                pltpu.VMEM((64, 2, 128), f32),
+                pltpu.VMEM((tops, 2, 128), f32),
+                pltpu.VMEM((4, 2, 128), f32),
                 pltpu.VMEM((512, 128), bf16),
                 pltpu.VMEM((512, 128), bf16),
                 pltpu.VMEM((1536, 128), bf16),

time: 29.6 us -> 28.9 us (0.976)
  Pallas kernels: 28.8 us -> 28.1 us
    pallas_call x1, Pallas kernels: 28.8 us -> 28.1 us  [body(): pl.pallas_call(functools.partial(kernel, tops, group, 8), out_shape=pltpu...]
where the time goes in v3:
time: 28.9 us; the launch traced here: 28.8 us
  Pallas kernels  28.1 us (97%)
  local copies, waits for them, and re-layouts  0.66 us (2%)
    pallas_call x1, Pallas kernels, body(): pl.pallas_call(functools.partial(kernel, tops, group, 8), out_shape=pltpu...  28.1 us
    unnamed x1, local copies, waits for them, and re-layouts  0.66 us

profile of v3, /device:TPU:1, one launch (start us, length us, event | category | flops | bytes accessed | tf_op | source)
XLA Modules:
  0.0 28.8 jit_solution(8634222124811009533)
XLA Ops:
  0.0 28.1 %h2.1 = f32[8,16,256]{2,1,0:T(8,128)S(1)} custom-call(bf16[8,16,256]{2,1,0:T(8,128)(2,1)} %bitcast.15, bf16[8,64,256]{2,1,0:T(8,128)(2,1)} %bitcast.13, f32[15,64,64]{2,1,0:T(8,128)} %bitcast.12, f32[36,64,64]{2,1,0:T(8,128)} %bitcast.11, f32[4,64,64]{2,1,0:T(8,128)} %bitcast.14, bf16[8,3,256,256]{3,2,1,0:T(8,128)(2,1)} %bitcast.10, s32[3,1,12]{2,1,0:T(1,128)} %bitcast.17, ...), custom_call_target="tpu_custom_call" | custom-call | tf_op jit(solution)/shard_map/h2/pallas_call | solution.py:363
  28.1 0.7 %copy.11 = f32[8,256,16]{1,2,0:T(8,128)} copy(f32[8,256,16]{1,2,0:T(8,128)S(1)} %bitcast.9) | data formatting | bytes 262144

commit v4 on v3

--- a/solution.py
+++ b/solution.py
@@ -10,7 +10,8 @@
 MESH = pl.DeviceIdType.MESH
 f32, bf16 = jnp.float32, jnp.bfloat16
 RELAY = 5
-OWNERS = 4
+OWNERS = 2
+ROWS = 8 // OWNERS
 NT = (((1,), (1,)), ((), ()))
 
 
@@ -166,8 +167,8 @@
         term = dot(twice(x), jnp.concatenate([high, high, low, low], axis=0))
         top = term if top is None else top + term
     packed = jnp.where(first8, top[0:8], top[8:16])
-    for i in range(4):
-        lifted_rows[i] = packed[2 * i : 2 * i + 2]
+    for i in range(OWNERS):
+        lifted_rows[i] = packed[ROWS * i : ROWS * (i + 1)]
 
     pl.semaphore_wait(
         barrier, 2 + side * OWNERS + jnp.where(owner, group - OWNERS - 1 + targets, 0)
@@ -237,7 +238,7 @@
     def _():
         others = parts_in.at[pl.ds(0, plane - 1)]
         pltpu.make_async_copy(others, others, sum_recv).wait()
-        tops_in[pl.ds(row_at * side, side)] = parts_in[...].reshape(side, group, 2, 128).sum(axis=1)
+        tops_in[pl.ds(row_at * side, side)] = parts_in[...].reshape(side, group, ROWS, 128).sum(axis=1)
         each_target(lambda z: pass_on(row_at, own_send.at[z], z).start())
 
     @pl.when(owner & (row_at == RELAY))
@@ -303,7 +304,7 @@
     def _():
         pltpu.make_async_copy(z_rows, z_rows, z_recv).wait()
 
-    z = jnp.concatenate([z_rows[i] for i in range(4)], axis=0)
+    z = jnp.concatenate([z_rows[i] for i in range(OWNERS)], axis=0)
     zero = jnp.zeros_like(z)
     z = jnp.concatenate([jnp.where(first8, z, zero), jnp.where(first8, zero, z)], axis=0)
     z_high, z_low = parts(z)
@@ -377,10 +378,10 @@
                 pltpu.SMEM((3, 8), jnp.int32),
                 pltpu.VMEM((14, 16, 128), bf16),
                 pltpu.VMEM((10, 16, 128), bf16),
-                pltpu.VMEM((4, 2, 128), f32),
-                pltpu.VMEM((64, 2, 128), f32),
-                pltpu.VMEM((tops, 2, 128), f32),
-                pltpu.VMEM((4, 2, 128), f32),
+                pltpu.VMEM((OWNERS, ROWS, 128), f32),
+                pltpu.VMEM((64, ROWS, 128), f32),
+                pltpu.VMEM((tops, ROWS, 128), f32),
+                pltpu.VMEM((OWNERS, ROWS, 128), f32),
                 pltpu.VMEM((512, 128), bf16),
                 pltpu.VMEM((512, 128), bf16),
                 pltpu.VMEM((1536, 128), bf16),

time: 28.9 us -> 28.6 us (0.990)
  Pallas kernels: 28.1 us -> 27.6 us
    pallas_call x1, Pallas kernels: 28.1 us -> 27.6 us  [body(): pl.pallas_call(functools.partial(kernel, tops, group, 8), out_shape=pltpu...]
where the time goes in v4:
time: 28.6 us; the launch traced here: 28.2 us
  Pallas kernels  27.6 us (97%)
  local copies, waits for them, and re-layouts  0.66 us (2%)
    pallas_call x1, Pallas kernels, body(): pl.pallas_call(functools.partial(kernel, tops, group, 8), out_shape=pltpu...  27.6 us
    unnamed x1, local copies, waits for them, and re-layouts  0.66 us

profile of v4, /device:TPU:1, one launch (start us, length us, event | category | flops | bytes accessed | tf_op | source)
XLA Modules:
  0.0 28.2 jit_solution(10640756902947749935)
XLA Ops:
  0.0 27.6 %h2.1 = f32[8,16,256]{2,1,0:T(8,128)S(1)} custom-call(bf16[8,16,256]{2,1,0:T(8,128)(2,1)} %bitcast.15, bf16[8,64,256]{2,1,0:T(8,128)(2,1)} %bitcast.13, f32[15,64,64]{2,1,0:T(8,128)} %bitcast.12, f32[36,64,64]{2,1,0:T(8,128)} %bitcast.11, f32[4,64,64]{2,1,0:T(8,128)} %bitcast.14, bf16[8,3,256,256]{3,2,1,0:T(8,128)(2,1)} %bitcast.10, s32[3,1,12]{2,1,0:T(1,128)} %bitcast.17, ...), custom_call_target="tpu_custom_call" | custom-call | tf_op jit(solution)/shard_map/h2/pallas_call | solution.py:364
  27.6 0.7 %copy.11 = f32[8,256,16]{1,2,0:T(8,128)} copy(f32[8,256,16]{1,2,0:T(8,128)S(1)} %bitcast.9) | data formatting | bytes 262144
